TPU v7x, 256 devices: a whole 4x4x8 slice. The times are simulated.
256 devices in a mesh: dp: 8 (over z), expert: 32 (over x, y, core).
Axes of the slice: x: 4, y: 4, z: 8, core: 2. Of those that a mesh axis runs over, the one named last changes fastest.
Arguments:
- tokens: bfloat16 [2048, 7168], P('expert', 'dp'), may hold values from -6 to 6
- tangent: bfloat16 [2048, 7168], P('expert', 'dp'), may hold values from -6 to 6
- cotangent: bfloat16 [2048, 7168], P('expert', 'dp'), may hold values from -3 to 3
- routing: int32 [2048, 8], P('expert'), may hold values from 0 to 31, all different within a row; in each aligned block of 64 rows (0 to 63, 64 to 127, ...) at most 18 rows name the same one
- gate_weights: float32 [2048, 8], P('expert'), may hold values from 0.1 to 0.6
- gate_proj: bfloat16 [32, 7168, 2048], P('expert', 'dp'), may hold values from -0.0625 to 0.0625
- up_proj: bfloat16 [32, 7168, 2048], P('expert', 'dp'), may hold values from -0.0625 to 0.0625
- down_proj: bfloat16 [32, 2048, 7168], P('expert', None, 'dp'), may hold values from -0.125 to 0.125
Outputs:
- hessian_product: float32 [2048, 7168], P('expert', 'dp')
Inputs may be any that keep to these rules, and one draw needn't show every extreme that they name: `routing`: each token names 8 different experts. In each aligned block of 64 tokens (the tokens of one index of expert) no expert is named more than 18 times, a bound that some block reaches.
All inputs are finite; a program needn't handle non-finite values.
Results may differ from a plain program's by a relative error of at most 0.0041.
Values may be sent and summed in bfloat16 or wider, within the bound.
A program may use at most 128 MiB of HBM per device.

v0:
```python
import jax
import jax.numpy as jnp
from jax import lax
from jax.sharding import PartitionSpec as P

TOP = 8


def second_order(pre_gate, pre_up, tangent_gate, tangent_up, back_hidden):
    sigma = jax.nn.sigmoid(pre_gate)
    first_slope = sigma * (1.0 + pre_gate * (1.0 - sigma))
    second_slope = sigma * (1.0 - sigma) * (2.0 + pre_gate * (1.0 - 2.0 * sigma))
    factor_a = back_hidden * (second_slope * tangent_gate * pre_up + first_slope * tangent_up)
    factor_b = back_hidden * first_slope * tangent_gate
    return (factor_a.astype(jnp.bfloat16), factor_b.astype(jnp.bfloat16))


def contract_last(left_rows, right_matrix):
    return lax.dot_general(
        left_rows, right_matrix, (((1,), (1,)), ((), ())), preferred_element_type=jnp.float32
    )


def shards(tokens, tangent, cotangent, routing, gate_weights, gate_proj, up_proj, down_proj):
    expert_count = lax.axis_size("expert")
    tok_rows = tokens.shape[0]
    feat_cols = tokens.shape[1]
    capacity = min(tok_rows, tok_rows * TOP // expert_count * 9 // 8)
    slot_total = expert_count * capacity
    routed_flat = routing.reshape(-1)
    route_hits = (
        routed_flat[:, None] == jnp.arange(expert_count, dtype=jnp.int32)[None, :]
    ).astype(jnp.int32)
    slot_index = jnp.sum((jnp.cumsum(route_hits, axis=0) - route_hits) * route_hits, axis=1)
    target_row = routed_flat * capacity + slot_index

    def scatter_rows(values):
        spread = jnp.repeat(values, TOP, axis=0)
        zero_buf = jnp.zeros((slot_total, values.shape[1]), values.dtype)
        return zero_buf.at[target_row].set(spread).reshape(expert_count, capacity, values.shape[1])

    x_rows = lax.all_to_all(
        scatter_rows(tokens), "expert", split_axis=0, concat_axis=0, tiled=True
    ).reshape(slot_total, feat_cols)
    paired = jnp.concatenate([tangent, cotangent], axis=1)
    paired_rows = lax.all_to_all(
        scatter_rows(paired), "expert", split_axis=0, concat_axis=0, tiled=True
    ).reshape(slot_total, 2 * feat_cols)
    v_rows = paired_rows[:, :feat_cols]
    c_rows = paired_rows[:, feat_cols:]
    gate_cols = gate_proj[0]
    up_cols = up_proj[0]
    down_rows = down_proj[0]
    part_gate = jnp.dot(x_rows, gate_cols, preferred_element_type=jnp.float32)
    part_up = jnp.dot(x_rows, up_cols, preferred_element_type=jnp.float32)
    part_tgate = jnp.dot(v_rows, gate_cols, preferred_element_type=jnp.float32)
    part_tup = jnp.dot(v_rows, up_cols, preferred_element_type=jnp.float32)
    part_back = contract_last(c_rows, down_rows)
    summed = (
        lax.psum_scatter(part_gate, "dp", scatter_dimension=0, tiled=True),
        lax.psum_scatter(part_up, "dp", scatter_dimension=0, tiled=True),
        lax.psum_scatter(part_tgate, "dp", scatter_dimension=0, tiled=True),
        lax.psum_scatter(part_tup, "dp", scatter_dimension=0, tiled=True),
        lax.psum_scatter(part_back, "dp", scatter_dimension=0, tiled=True),
    )
    factor_a, factor_b = second_order(summed[0], summed[1], summed[2], summed[3], summed[4])
    factors = jnp.stack([factor_a, factor_b])
    piece = lax.all_gather(factors, "dp", axis=1, tiled=True)
    result_rows = contract_last(piece[0], gate_cols) + contract_last(piece[1], up_cols)
    outgoing = result_rows.astype(jnp.bfloat16).reshape(expert_count, capacity, feat_cols)
    returned = lax.all_to_all(outgoing, "expert", split_axis=0, concat_axis=0, tiled=True).reshape(
        slot_total, feat_cols
    )
    gathered = returned[target_row].reshape(tok_rows, TOP, feat_cols).astype(jnp.float32)
    return jnp.sum(gate_weights[:, :, None] * gathered, axis=1)


def solution(mesh):
    in_specs = (
        P("expert", "dp"),
        P("expert", "dp"),
        P("expert", "dp"),
        P("expert", None),
        P("expert", None),
        P("expert", "dp", None),
        P("expert", "dp", None),
        P("expert", None, "dp"),
    )
    out_specs = P("expert", "dp")
    return jax.shard_map(shards, mesh=mesh, in_specs=in_specs, out_specs=out_specs, check_vma=False)
```

profile of v0, /device:TPU:1, one launch (start us, length us, event | category | flops | bytes accessed | tf_op | source)
XLA Modules:
  0.0 463.8 jit_solution(245255507557251218)
XLA Ops:
  6.5 0.0 copy-start
  6.5 0.0 reduce-scatter.12.cloned.1.call-start
  6.5 0.8 copy.12
  7.3 0.1 eq.29
  7.4 0.1 eq.25
  7.5 0.7 broadcast_multiply_fusion
  8.2 1.2 reduce-window.6
  9.4 0.2 slice_reduce_fusion
  9.7 0.1 copy.11
  9.7 0.1 mul.66
  9.8 0.1 fusion.40
  10.0 0.0 copy-done
  10.0 3.0 scatter_custom_fusion.1
  12.9 0.3 reshape.79
  13.3 29.3 %all_to_all.15 = bf16[32,18,896]{2,1,0:T(8,128)(2,1)S(1)} all-to-all(bf16[32,18,896]{2,1,0:T(8,128)(2,1)S(1)} %reshape.79), channel_id=1, replica_groups=mesh['dp'=8,'expert'=32] {'expert'}, dimensions={0} | all-to-all | bytes 2064384 | tf_op jit(solution)/shard_map/all_to_all | solution.py:42
  42.6 0.3 reshape.80
  42.9 6.3 %fusion.4 = f32[576,2048]{1,0:T(8,128)} fusion(bf16[576,896]{1,0:T(8,128)(2,1)S(1)} %reshape.80, bf16[1,896,2048]{2,1,0:T(8,128)(2,1)} %param.14), kind=kOutput, calls=%fused_computation.7 | convolution fusion | flops 2113929216 | bytes 9420800 | tf_op jit(solution)/shard_map/dot_general | solution.py:55
  49.2 0.0 reduce-scatter.12.cloned.1.call-update
  49.2 0.0 reduce-scatter.8.cloned.1.call-start
  49.3 6.3 %fusion.10 = f32[576,2048]{1,0:T(8,128)} fusion(bf16[576,896]{1,0:T(8,128)(2,1)S(1)} %reshape.80, bf16[1,896,2048]{2,1,0:T(8,128)(2,1)} %param.13), kind=kOutput, calls=%fused_computation.13 | convolution fusion | flops 2113929216 | bytes 9420800 | tf_op jit(solution)/shard_map/dot_general | solution.py:54
  55.6 0.0 copy-start.1
  55.6 0.0 copy-start.2
  55.6 0.0 reduce-scatter.8.cloned.1.call-update
  55.6 0.0 reduce-scatter.10.cloned.1.call-start
  55.7 0.8 copy-done.1
  56.5 0.1 copy-done.2
  56.6 4.8 %scatter_custom_fusion = bf16[576,1792]{1,0:T(8,128)(2,1)} fusion(s32[512]{0:T(512)S(1)} %bitcast.64, bf16[]{:T(256)} %constant.7.clone.1, bf16[64,1792]{1,0:T(8,128)(2,1)S(1)} %pad_maximum_fusion.1), kind=kCustom, calls=%fused_computation.22 | custom fusion | bytes 2293762 | tf_op jit(solution)/shard_map/scatter | solution.py:40
  61.4 2.6 reshape.76
  64.0 39.1 %all_to_all.16 = bf16[32,18,1792]{2,1,0:T(8,128)(2,1)} all-to-all(bf16[32,18,1792]{2,1,0:T(8,128)(2,1)S(1)} %reshape.76), channel_id=1, replica_groups=mesh['dp'=8,'expert'=32] {'expert'}, dimensions={0} | all-to-all | bytes 4128768 | tf_op jit(solution)/shard_map/all_to_all | solution.py:46
  103.1 2.8 reshape.77
  105.9 6.4 %fusion.8 = f32[576,2048]{1,0:T(8,128)} fusion(bf16[1,896,2048]{2,1,0:T(8,128)(2,1)} %param.13, bf16[576,1792]{1,0:T(8,128)(2,1)S(1)} %reshape.77), kind=kOutput, calls=%fused_computation.11 | convolution fusion | flops 2113929216 | bytes 9420800 | tf_op jit(solution)/shard_map/dot_general | solution.py:56
  112.3 0.0 reduce-scatter.10.cloned.1.call-update
  112.3 0.2 reduce-scatter.14.cloned.1.call-start
  112.6 6.3 %fusion.2 = f32[576,2048]{1,0:T(8,128)} fusion(bf16[1,896,2048]{2,1,0:T(8,128)(2,1)} %param.14, bf16[576,1792]{1,0:T(8,128)(2,1)S(1)} %reshape.77), kind=kOutput, calls=%fused_computation.5 | convolution fusion | flops 2113929216 | bytes 9420800 | tf_op jit(solution)/shard_map/dot_general | solution.py:57
  118.8 0.0 reduce-scatter.14.cloned.1.call-update
  118.9 0.0 reduce-scatter.6.cloned.1.call-start
  118.9 6.4 %fusion.12 = f32[576,2048]{1,0:T(8,128)} fusion(bf16[1,2048,896]{2,1,0:T(8,128)(2,1)} %param.15, bf16[576,1792]{1,0:T(8,128)(2,1)S(1)} %reshape.77), kind=kOutput, calls=%fused_computation.15 | convolution fusion | flops 2113929216 | bytes 9420800 | tf_op jit(solution)/shard_map/dot_general | solution.py:19
  125.3 0.0 reduce-scatter.6.cloned.1.call-update
  125.3 0.0 all-gather.2.cloned.1.call-start
  125.4 0.0 reduce-scatter.12.cloned.1.call-done
  125.4 44.6 %reduce-scatter.8.cloned.1.call-done = f32[72,2048]{1,0:T(8,128)} async-done(((f32[576,2048]{1,0:T(8,128)}), f32[72,2048]{1,0:T(8,128)}) %reduce-scatter.8.cloned.1.call-update) | async-done | bytes 589840 | tf_op jit(solution)/shard_map/reduce_scatter | solution.py:60
  170.0 61.5 %reduce-scatter.10.cloned.1.call-done = f32[72,2048]{1,0:T(8,128)} async-done(((f32[576,2048]{1,0:T(8,128)}), f32[72,2048]{1,0:T(8,128)}) %reduce-scatter.10.cloned.1.call-update) | async-done | bytes 589840 | tf_op jit(solution)/shard_map/reduce_scatter | solution.py:62
  231.5 61.3 %reduce-scatter.14.cloned.1.call-done = f32[72,2048]{1,0:T(8,128)} async-done(((f32[576,2048]{1,0:T(8,128)}), f32[72,2048]{1,0:T(8,128)}) %reduce-scatter.14.cloned.1.call-update) | async-done | bytes 589840 | tf_op jit(solution)/shard_map/reduce_scatter | solution.py:63
  292.8 61.3 %reduce-scatter.6.cloned.1.call-done = f32[72,2048]{1,0:T(8,128)} async-done(((f32[576,2048]{1,0:T(8,128)}), f32[72,2048]{1,0:T(8,128)}) %reduce-scatter.6.cloned.1.call-update) | async-done | bytes 589840 | tf_op jit(solution)/shard_map/reduce_scatter | solution.py:64
  354.1 2.2 fusion.37
  356.3 0.9 pad_maximum_fusion
  357.2 0.0 all-gather.2.cloned.1.call-update
  357.2 58.5 %all-gather.2.cloned.1.call-done = bf16[2,576,2048]{2,1,0:T(8,128)(2,1)} async-done(((bf16[2,72,2048]{2,1,0:T(8,128)(2,1)}), bf16[2,576,2048]{2,1,0:T(8,128)(2,1)}) %all-gather.2.cloned.1.call-update) | async-done | bytes 4718608 | tf_op jit(solution)/shard_map/all_gather | solution.py:68
  415.7 0.0 copy-start.4
  415.7 0.0 copy-start.5
  415.7 5.5 %fusion = f32[576,896]{1,0:T(8,128)S(1)} fusion(bf16[1,896,2048]{2,1,0:T(8,128)(2,1)} %param.14, bf16[2,576,2048]{2,1,0:T(8,128)(2,1)} %all-gather.2.cloned.1.call-done), kind=kOutput, calls=%fused_computation.3 | convolution fusion | flops 2113929216 | bytes 8093696 | tf_op jit(solution)/shard_map/dot_general | solution.py:19
  421.2 0.0 copy-done.4
  421.2 0.0 copy-done.5
  421.3 2.7 add_convert_fusion
  423.9 0.0 copy-start.3
  423.9 1.3 reshape.81
  425.2 7.5 %all-to-all-start.2 = ((bf16[32,18,896]{2,1,0:T(8,128)(2,1)}), bf16[32,18,896]{2,1,0:T(8,128)(2,1)S(1)}, u32[]{:S(2)}, u32[]{:S(2)}) async-start(bf16[32,18,896]{2,1,0:T(8,128)(2,1)} %reshape.81), calls=%async_computation.7 | async-start | bytes 2752512 | tf_op jit(solution)/shard_map/all_to_all | solution.py:71
  432.7 0.0 copy-done.3
  432.7 0.1 copy.10
  432.8 20.4 %all-to-all-done.2 = bf16[32,18,896]{2,1,0:T(8,128)(2,1)S(1)} async-done(((bf16[32,18,896]{2,1,0:T(8,128)(2,1)}), bf16[32,18,896]{2,1,0:T(8,128)(2,1)S(1)}, u32[]{:S(2)}, u32[]{:S(2)}) %all-to-all-start.2) | async-done | bytes 1032224 | tf_op jit(solution)/shard_map/all_to_all | solution.py:71
  453.2 0.3 reshape.82
  453.6 2.1 gather_fusion
  455.6 1.3 fusion.14
  (6 shorter events, 0.1 us)
Async XLA Ops:
  6.5 3.4 copy-start
  6.5 118.8 %reduce-scatter.12.cloned.1.call-start = ((), (), s32[]{:S(2)}) async-start(), calls=%async_computation.11 | async-start | bytes 5308416 | tf_op jit(solution)/shard_map/reduce_scatter | solution.py:61
  49.2 120.8 %reduce-scatter.8.cloned.1.call-start = ((), (), s32[]{:S(2)}) async-start(), calls=%async_computation.9 | async-start | bytes 5308416 | tf_op jit(solution)/shard_map/reduce_scatter | solution.py:60
  55.6 0.9 copy-start.1
  55.6 1.0 copy-start.2
  55.6 175.8 %reduce-scatter.10.cloned.1.call-start = ((), (), s32[]{:S(2)}) async-start(), calls=%async_computation.10 | async-start | bytes 5308416 | tf_op jit(solution)/shard_map/reduce_scatter | solution.py:62
  112.3 180.5 %reduce-scatter.14.cloned.1.call-start = ((), (), s32[]{:S(2)}) async-start(), calls=%async_computation.12 | async-start | bytes 5308416 | tf_op jit(solution)/shard_map/reduce_scatter | solution.py:63
  118.9 235.2 %reduce-scatter.6.cloned.1.call-start = ((), (), s32[]{:S(2)}) async-start(), calls=%async_computation.8 | async-start | bytes 5308416 | tf_op jit(solution)/shard_map/reduce_scatter | solution.py:64
  125.3 290.4 %all-gather.2.cloned.1.call-start = ((), (), s32[]{:S(2)}) async-start(), calls=%async_computation.13 | async-start | bytes 5308416 | tf_op jit(solution)/shard_map/all_gather | solution.py:68
  415.7 5.5 %copy-start.4 = (bf16[2,576,2048]{2,1,0:T(8,128)(2,1)S(1)}, bf16[2,576,2048]{2,1,0:T(8,128)(2,1)}, u32[]{:S(2)}) copy-start(bf16[2,576,2048]{2,1,0:T(8,128)(2,1)} %all-gather.2.cloned.1.call-done) | copy-start | bytes 14155780
  415.7 5.5 %copy-start.5 = (bf16[1,896,2048]{2,1,0:T(8,128)(2,1)S(1)}, bf16[1,896,2048]{2,1,0:T(8,128)(2,1)}, u32[]{:S(2)}) copy-start(bf16[1,896,2048]{2,1,0:T(8,128)(2,1)} %param.13) | copy-start | bytes 11010052
  423.9 8.8 %copy-start.3 = (f32[64,8]{0,1:T(8,128)S(1)}, f32[64,8]{0,1:T(8,128)}, u32[]{:S(2)}) copy-start(f32[64,8]{0,1:T(8,128)} %param.12) | copy-start | bytes 6148
  425.2 28.0 %all-to-all-start.2 = ((bf16[32,18,896]{2,1,0:T(8,128)(2,1)}), bf16[32,18,896]{2,1,0:T(8,128)(2,1)S(1)}, u32[]{:S(2)}, u32[]{:S(2)}) async-start(bf16[32,18,896]{2,1,0:T(8,128)(2,1)} %reshape.81), calls=%async_computation.7 | async-start | bytes 2752512 | tf_op jit(solution)/shard_map/all_to_all | solution.py:71
Sparse Core Ops, SparseCore 0:
  49.3 59.1 reduce-scatter.11
  111.0 58.8 reduce-scatter.7
  172.5 58.8 reduce-scatter.9
  233.9 58.8 reduce-scatter.13
  295.2 58.8 reduce-scatter.5
  357.3 58.3 all-gather.1
where the time goes:
time: 464 us
  waiting for transfers between devices  308 us (66%)
  blocking collectives  68.4 us (15%)
  matrix products  39.8 us (9%)
  local copies, waits for them, and re-layouts  19.9 us (4%)
  between operations  13.6 us (3%)
  starting transfers between devices  7.92 us (2%)
  other arithmetic  6.42 us (1%)
    reduce_scatter x1, waiting for transfers between devices, shards(): lax.psum_scatter(part_tgate, 'dp', scatter_dimension=0, tiled=True)  61.5 us
    reduce_scatter x1, waiting for transfers between devices, shards(): lax.psum_scatter(part_tup, 'dp', scatter_dimension=0, tiled=True)  61.3 us
    reduce_scatter x1, waiting for transfers between devices, shards(): lax.psum_scatter(part_back, 'dp', scatter_dimension=0, tiled=True)  61.3 us
    all_gather x1, waiting for transfers between devices, shards(): piece = lax.all_gather(factors, 'dp', axis=1, tiled=True)  58.5 us
    reduce_scatter x1, waiting for transfers between devices, shards(): lax.psum_scatter(part_gate, 'dp', scatter_dimension=0, tiled=True)  44.6 us
    all_to_all x1, blocking collectives, shards(): lax.all_to_all(scatter_rows(paired), 'expert', split_axis=0, concat_axis=...  39.1 us
    all_to_all x1, blocking collectives, shards(): lax.all_to_all(scatter_rows(tokens), 'expert', split_axis=0, concat_axis=...  29.3 us
    all_to_all x1, waiting for transfers between devices, shards(): lax.all_to_all(outgoing, 'expert', split_axis=0, concat_axis=0, tiled=True)  20.4 us
  transfers between devices with their start and end apart: 7, of which 6 were waited for; matrix products, arithmetic and copies ran while one was open for 8% of the time, Pallas kernels for 0%

commit v1 on v0

--- a/solution.py
+++ b/solution.py
@@ -65,7 +65,9 @@
     )
     factor_a, factor_b = second_order(summed[0], summed[1], summed[2], summed[3], summed[4])
     factors = jnp.stack([factor_a, factor_b])
-    piece = lax.all_gather(factors, "dp", axis=1, tiled=True)
+    piece = jnp.concatenate(
+        lax.all_to_all(jnp.stack([factors] * lax.axis_size("dp")), "dp", 0, 0), axis=1
+    )
     result_rows = contract_last(piece[0], gate_cols) + contract_last(piece[1], up_cols)
     outgoing = result_rows.astype(jnp.bfloat16).reshape(expert_count, capacity, feat_cols)
     returned = lax.all_to_all(outgoing, "expert", split_axis=0, concat_axis=0, tiled=True).reshape(

time: 464 us -> 516 us (1.11)
  blocking collectives: 68.4 us -> 178 us
  waiting for transfers between devices: 308 us -> 249 us
    all_to_all x0 -> x1, blocking collectives: none -> 110 us  [shards(): lax.all_to_all(jnp.stack([factors] * lax.axis_size('dp')), 'dp', 0, 0)]
    all_gather x1 -> x0, waiting for transfers between devices: 58.5 us -> none  [shards(): piece = lax.all_gather(factors, 'dp', axis=1, tiled=True)]
  transfers between devices with their start and end apart: 7 -> 6, of which waited for: 6 -> 5; matrix products, arithmetic and copies ran while one was open for 8% -> 7% of each run, Pallas kernels for 0% -> 0%
where the time goes in v1:
time: 516 us; the launch traced here: 515 us
  waiting for transfers between devices  249 us (48%)
  blocking collectives  178 us (34%)
  matrix products  36.9 us (7%)
  local copies, waits for them, and re-layouts  22.5 us (4%)
  between operations  13.3 us (3%)
  starting transfers between devices  9.55 us (2%)
  other arithmetic  5.59 us (1%)
    all_to_all x1, blocking collectives, shards(): lax.all_to_all(jnp.stack([factors] * lax.axis_size('dp')), 'dp', 0, 0)  110 us
    reduce_scatter x1, waiting for transfers between devices, shards(): lax.psum_scatter(part_tgate, 'dp', scatter_dimension=0, tiled=True)  61.5 us
    reduce_scatter x1, waiting for transfers between devices, shards(): lax.psum_scatter(part_back, 'dp', scatter_dimension=0, tiled=True)  61.3 us
    reduce_scatter x1, waiting for transfers between devices, shards(): lax.psum_scatter(part_tup, 'dp', scatter_dimension=0, tiled=True)  61.3 us
    reduce_scatter x1, waiting for transfers between devices, shards(): lax.psum_scatter(part_gate, 'dp', scatter_dimension=0, tiled=True)  44.6 us
    all_to_all x1, blocking collectives, shards(): lax.all_to_all(scatter_rows(paired), 'expert', split_axis=0, concat_axis=...  39.1 us
    all_to_all x1, blocking collectives, shards(): lax.all_to_all(scatter_rows(tokens), 'expert', split_axis=0, concat_axis=...  29.3 us
    all_to_all x1, waiting for transfers between devices, shards(): lax.all_to_all(outgoing, 'expert', split_axis=0, concat_axis=0, tiled=True)  20.4 us
  transfers between devices with their start and end apart: 6, of which 5 were waited for; matrix products, arithmetic and copies ran while one was open for 7% of the time, Pallas kernels for 0%

profile of v1, /device:TPU:1, one launch (start us, length us, event | category | flops | bytes accessed | tf_op | source)
XLA Modules:
  0.0 515.4 jit_solution(7727833547130050697)
XLA Ops:
  6.5 0.0 copy-start
  6.5 0.0 reduce-scatter.12.cloned.1.call-start
  6.5 0.8 copy.12
  7.3 0.1 eq.29
  7.4 0.1 eq.25
  7.5 0.7 broadcast_multiply_fusion
  8.2 1.2 reduce-window.6
  9.4 0.2 slice_reduce_fusion
  9.7 0.1 copy.11
  9.7 0.1 mul.66
  9.8 0.1 fusion.40
  10.0 0.0 copy-done
  10.0 3.0 scatter_custom_fusion.1
  12.9 0.3 reshape.89
  13.3 29.3 %all_to_all.20 = bf16[32,18,896]{2,1,0:T(8,128)(2,1)S(1)} all-to-all(bf16[32,18,896]{2,1,0:T(8,128)(2,1)S(1)} %reshape.89), channel_id=1, replica_groups=mesh['dp'=8,'expert'=32] {'expert'}, dimensions={0} | all-to-all | bytes 2064384 | tf_op jit(solution)/shard_map/all_to_all | solution.py:42
  42.6 0.3 reshape.90
  42.9 6.3 %fusion.4 = f32[576,2048]{1,0:T(8,128)} fusion(bf16[576,896]{1,0:T(8,128)(2,1)S(1)} %reshape.90, bf16[1,896,2048]{2,1,0:T(8,128)(2,1)} %param.14), kind=kOutput, calls=%fused_computation.7 | convolution fusion | flops 2113929216 | bytes 9420800 | tf_op jit(solution)/shard_map/dot_general | solution.py:55
  49.2 0.0 reduce-scatter.12.cloned.1.call-update
  49.2 0.0 reduce-scatter.8.cloned.1.call-start
  49.3 6.3 %fusion.10 = f32[576,2048]{1,0:T(8,128)} fusion(bf16[576,896]{1,0:T(8,128)(2,1)S(1)} %reshape.90, bf16[1,896,2048]{2,1,0:T(8,128)(2,1)} %param.13), kind=kOutput, calls=%fused_computation.13 | convolution fusion | flops 2113929216 | bytes 9420800 | tf_op jit(solution)/shard_map/dot_general | solution.py:54
  55.6 0.0 copy-start.2
  55.6 0.0 copy-start.3
  55.6 0.0 reduce-scatter.8.cloned.1.call-update
  55.6 0.0 reduce-scatter.10.cloned.1.call-start
  55.7 0.8 copy-done.2
  56.5 0.1 copy-done.3
  56.6 4.8 scatter_custom_fusion
  61.4 2.6 reshape.86
  64.0 39.1 %all_to_all.21 = bf16[32,18,1792]{2,1,0:T(8,128)(2,1)} all-to-all(bf16[32,18,1792]{2,1,0:T(8,128)(2,1)S(1)} %reshape.86), channel_id=1, replica_groups=mesh['dp'=8,'expert'=32] {'expert'}, dimensions={0} | all-to-all | bytes 4128768 | tf_op jit(solution)/shard_map/all_to_all | solution.py:46
  103.1 2.8 reshape.87
  105.9 6.4 %fusion.8 = f32[576,2048]{1,0:T(8,128)} fusion(bf16[1,896,2048]{2,1,0:T(8,128)(2,1)} %param.13, bf16[576,1792]{1,0:T(8,128)(2,1)S(1)} %reshape.87), kind=kOutput, calls=%fused_computation.11 | convolution fusion | flops 2113929216 | bytes 9420800 | tf_op jit(solution)/shard_map/dot_general | solution.py:56
  112.3 0.0 reduce-scatter.10.cloned.1.call-update
  112.3 0.2 reduce-scatter.14.cloned.1.call-start
  112.6 6.3 %fusion.2 = f32[576,2048]{1,0:T(8,128)} fusion(bf16[1,896,2048]{2,1,0:T(8,128)(2,1)} %param.14, bf16[576,1792]{1,0:T(8,128)(2,1)S(1)} %reshape.87), kind=kOutput, calls=%fused_computation.5 | convolution fusion | flops 2113929216 | bytes 9420800 | tf_op jit(solution)/shard_map/dot_general | solution.py:57
  118.8 0.0 reduce-scatter.14.cloned.1.call-update
  118.9 0.0 reduce-scatter.6.cloned.1.call-start
  118.9 6.4 %fusion.12 = f32[576,2048]{1,0:T(8,128)} fusion(bf16[1,2048,896]{2,1,0:T(8,128)(2,1)} %param.15, bf16[576,1792]{1,0:T(8,128)(2,1)S(1)} %reshape.87), kind=kOutput, calls=%fused_computation.15 | convolution fusion | flops 2113929216 | bytes 9420800 | tf_op jit(solution)/shard_map/dot_general | solution.py:19
  125.3 0.0 reduce-scatter.6.cloned.1.call-update
  125.3 0.0 reduce-scatter.12.cloned.1.call-done
  125.3 44.6 %reduce-scatter.8.cloned.1.call-done = f32[72,2048]{1,0:T(8,128)} async-done(((f32[576,2048]{1,0:T(8,128)}), f32[72,2048]{1,0:T(8,128)}) %reduce-scatter.8.cloned.1.call-update) | async-done | bytes 589840 | tf_op jit(solution)/shard_map/reduce_scatter | solution.py:60
  170.0 61.5 %reduce-scatter.10.cloned.1.call-done = f32[72,2048]{1,0:T(8,128)} async-done(((f32[576,2048]{1,0:T(8,128)}), f32[72,2048]{1,0:T(8,128)}) %reduce-scatter.10.cloned.1.call-update) | async-done | bytes 589840 | tf_op jit(solution)/shard_map/reduce_scatter | solution.py:62
  231.5 61.3 %reduce-scatter.14.cloned.1.call-done = f32[72,2048]{1,0:T(8,128)} async-done(((f32[576,2048]{1,0:T(8,128)}), f32[72,2048]{1,0:T(8,128)}) %reduce-scatter.14.cloned.1.call-update) | async-done | bytes 589840 | tf_op jit(solution)/shard_map/reduce_scatter | solution.py:63
  292.8 61.3 %reduce-scatter.6.cloned.1.call-done = f32[72,2048]{1,0:T(8,128)} async-done(((f32[576,2048]{1,0:T(8,128)}), f32[72,2048]{1,0:T(8,128)}) %reduce-scatter.6.cloned.1.call-update) | async-done | bytes 589840 | tf_op jit(solution)/shard_map/reduce_scatter | solution.py:64
  354.1 2.2 fusion.37
  356.3 0.1 pad_maximum_fusion
  356.4 0.6 stack.11
  357.0 109.8 %all_to_all.22 = bf16[8,2,72,2048]{3,2,1,0:T(8,128)(2,1)S(1)} all-to-all(bf16[8,2,72,2048]{3,2,1,0:T(8,128)(2,1)S(1)} %stack.11), channel_id=1, replica_groups=mesh['dp'=8,'expert'=32] {'dp'}, dimensions={0} | all-to-all | bytes 9437184 | tf_op jit(solution)/shard_map/all_to_all | solution.py:69
  466.8 0.0 copy-start.5
  466.8 0.7 fusion.42
  467.5 1.3 copy-done.5
  468.9 2.6 fusion
  471.5 0.0 copy-done.6
  471.5 2.7 add_convert_fusion
  474.2 0.0 copy-start.4
  474.2 1.3 reshape.92
  475.4 9.2 %all-to-all-start.3 = ((bf16[32,18,896]{2,1,0:T(8,128)(2,1)}), bf16[32,18,896]{2,1,0:T(8,128)(2,1)S(1)}, u32[]{:S(2)}, u32[]{:S(2)}) async-start(bf16[32,18,896]{2,1,0:T(8,128)(2,1)} %reshape.92), calls=%async_computation.8 | async-start | bytes 2752512 | tf_op jit(solution)/shard_map/all_to_all | solution.py:73
  484.6 0.0 copy-done.4
  484.7 0.1 copy.10
  484.8 20.4 %all-to-all-done.3 = bf16[32,18,896]{2,1,0:T(8,128)(2,1)S(1)} async-done(((bf16[32,18,896]{2,1,0:T(8,128)(2,1)}), bf16[32,18,896]{2,1,0:T(8,128)(2,1)S(1)}, u32[]{:S(2)}, u32[]{:S(2)}) %all-to-all-start.3) | async-done | bytes 1032224 | tf_op jit(solution)/shard_map/all_to_all | solution.py:73
  505.2 0.3 reshape.93
  505.5 0.0 copy-start.1
  505.5 2.1 gather_fusion
  507.6 1.3 fusion.14
  508.9 0.0 copy-done.1
  (7 shorter events, 0.1 us)
Async XLA Ops:
  6.5 3.4 copy-start
  6.5 118.8 %reduce-scatter.12.cloned.1.call-start = ((), (), s32[]{:S(2)}) async-start(), calls=%async_computation.12 | async-start | bytes 5308416 | tf_op jit(solution)/shard_map/reduce_scatter | solution.py:61
  49.2 120.8 %reduce-scatter.8.cloned.1.call-start = ((), (), s32[]{:S(2)}) async-start(), calls=%async_computation.10 | async-start | bytes 5308416 | tf_op jit(solution)/shard_map/reduce_scatter | solution.py:60
  55.6 0.9 copy-start.2
  55.6 1.0 copy-start.3
  55.6 175.8 %reduce-scatter.10.cloned.1.call-start = ((), (), s32[]{:S(2)}) async-start(), calls=%async_computation.11 | async-start | bytes 5308416 | tf_op jit(solution)/shard_map/reduce_scatter | solution.py:62
  112.3 180.4 %reduce-scatter.14.cloned.1.call-start = ((), (), s32[]{:S(2)}) async-start(), calls=%async_computation.13 | async-start | bytes 5308416 | tf_op jit(solution)/shard_map/reduce_scatter | solution.py:63
  118.9 235.2 %reduce-scatter.6.cloned.1.call-start = ((), (), s32[]{:S(2)}) async-start(), calls=%async_computation.9 | async-start | bytes 5308416 | tf_op jit(solution)/shard_map/reduce_scatter | solution.py:64
  466.8 2.0 copy-start.5
  468.9 2.6 copy-start.6
  474.2 10.5 %copy-start.4 = (f32[64,8]{0,1:T(8,128)S(1)}, f32[64,8]{0,1:T(8,128)}, u32[]{:S(2)}) copy-start(f32[64,8]{0,1:T(8,128)} %param.12) | copy-start | bytes 6148
  475.4 29.7 %all-to-all-start.3 = ((bf16[32,18,896]{2,1,0:T(8,128)(2,1)}), bf16[32,18,896]{2,1,0:T(8,128)(2,1)S(1)}, u32[]{:S(2)}, u32[]{:S(2)}) async-start(bf16[32,18,896]{2,1,0:T(8,128)(2,1)} %reshape.92), calls=%async_computation.8 | async-start | bytes 2752512 | tf_op jit(solution)/shard_map/all_to_all | solution.py:73
  505.5 3.4 copy-start.1
Sparse Core Ops, SparseCore 0:
  49.3 59.1 reduce-scatter.11
  111.0 58.8 reduce-scatter.7
  172.5 58.8 reduce-scatter.9
  233.9 58.8 reduce-scatter.13
  295.2 58.8 reduce-scatter.5
